TPU v7x, 32 devices: a whole 2x2x4 slice. The times are simulated.
32 devices in a mesh: grp: 2 (over x), ep: 16 (over z, y, core).
Axes of the slice: x: 2, y: 2, z: 4, core: 2. Of those that a mesh axis runs over, the one named last changes fastest.
Arguments:
- tokens_one: bfloat16 [1024, 2048], P(('grp', 'ep')), may hold values from -6 to 6
- routes_one: int32 [1024, 6], P(('grp', 'ep')), may hold values from 0 to 15, all different within a row; in each aligned block of 32 rows (0 to 31, 32 to 63, ...) at most 18 rows name the same one
- gates_one: bfloat16 [1024, 6], P(('grp', 'ep')), may hold values from 0.049804688 to 0.3984375
- tokens_two: bfloat16 [1024, 2048], P(('grp', 'ep')), may hold values from -6 to 6
- routes_two: int32 [1024, 6], P(('grp', 'ep')), may hold values from 0 to 15, all different within a row; in each aligned block of 32 rows (0 to 31, 32 to 63, ...) at most 18 rows name the same one
- gates_two: bfloat16 [1024, 6], P(('grp', 'ep')), may hold values from 0.049804688 to 0.3984375
- old_table: int32 [16], replicated, may hold values from 0 to 15, each once
- new_table: int32 [16], replicated, may hold values from 0 to 15, each once
- gate_up: bfloat16 [16, 2048, 1408], P('ep'), may hold values from -0.125 to 0.125
- down_proj: bfloat16 [16, 704, 2048], P('ep'), may hold values from -0.21875 to 0.21875
- norm_gain: bfloat16 [2048], replicated, may hold values from 0.099609375 to 1.8984375
- kv_weight: bfloat16 [2048, 1024], P(None, 'grp'), may hold values from -0.125 to 0.125
Outputs:
- hidden_one: bfloat16 [1024, 2048], P(('grp', 'ep'))
- kv_one: bfloat16 [1024, 1024], P(('grp', 'ep'))
- hidden_two: bfloat16 [1024, 2048], P(('grp', 'ep'))
- kv_two: bfloat16 [1024, 1024], P(('grp', 'ep'))
- gate_up_new: bfloat16 [16, 2048, 1408], P('ep', 'grp')
- down_proj_new: bfloat16 [16, 704, 2048], P('ep', None, 'grp')
Inputs may be any that keep to these rules, and one draw needn't show every extreme that they name: `routes_one`: each row names 6 different slots; among the rows of one device no slot is named by more than 18 routes, a bound that some block reaches. `routes_two`: each row names 6 different slots; among the rows of one device no slot is named by more than 18 routes, a bound that some block reaches. `old_table`: each expert appears once. `new_table`: each expert appears once.
All inputs are finite; a program needn't handle non-finite values.
Results may differ from a plain program's by a relative error of at most 0.006.
Values may be sent and summed in bfloat16 or wider, within the bound.
No kernel may reach another device: no remote copies, remote signals or barrier semaphores. Data moves between devices by JAX's collectives and lax.ppermute only.
A program may use at most 128 MiB of HBM per device.

v0:
```python
import jax
import jax.numpy as jnp
from jax import lax
from jax.experimental import pallas as pl
from jax.experimental.pallas import tpu as pltpu
from jax.sharding import PartitionSpec as P

TOP = 6
LANES = 128
BF = jnp.bfloat16
F32 = jnp.float32


def rms_norm(hidden, norm_gain):
    values = hidden.astype(F32)
    inverse_rms = lax.rsqrt(jnp.mean(values * values, axis=-1, keepdims=True) + 1e-06)
    return (values * inverse_rms * norm_gain.astype(F32)).astype(BF)


def swap(x, axis, distance):
    size = lax.axis_size(axis)
    return lax.ppermute(x, axis, [(i, i ^ distance) for i in range(size)])


def join(parts):
    rows, feat = parts[0][0].shape

    def body(*refs):
        out = refs[-1]
        for i in range(len(parts)):
            tok, gat, rou = refs[3 * i : 3 * i + 3]
            out[i * rows : (i + 1) * rows, :feat] = tok[...]
            lane = lax.broadcasted_iota(jnp.int32, (TOP, LANES), 1)
            line = lax.broadcasted_iota(jnp.int32, (TOP, LANES), 0)
            more = sum(
                lax.dot_general(
                    x[...].astype(F32).astype(BF),
                    (lane == line + first).astype(F32).astype(BF),
                    (((0,), (0,)), ((), ())),
                    preferred_element_type=F32,
                )
                for x, first in ((gat, 0), (rou, TOP))
            )
            out[i * rows : (i + 1) * rows, feat:] = more.astype(BF)

    shape = (len(parts) * rows, feat + LANES)
    vmem = pl.BlockSpec(memory_space=pltpu.VMEM)
    return pl.pallas_call(
        body,
        name="join",
        out_shape=jax.ShapeDtypeStruct(shape, BF),
        in_specs=[vmem] * (3 * len(parts)),
        out_specs=vmem,
        cost_estimate=pl.CostEstimate(
            flops=0, bytes_accessed=4 * shape[0] * shape[1], transcendentals=0
        ),
    )(*[x for part in parts for x in part])


def experts(rows, each, targets, w_in, w_out, dtype):
    inner, feat = w_out.shape
    count = rows.shape[0]
    width = rows.shape[1]
    step = min(256, count)

    def body(target_ref, row_ref, in_ref, out_w_ref, out_ref):
        joined = jnp.dot(row_ref[:, :feat], in_ref[...], preferred_element_type=F32)
        upward = pltpu.roll(joined, inner, 1)
        hidden = joined / (1.0 + jnp.exp(-joined)) * upward
        hidden = hidden[:, :inner].astype(BF)
        result = jnp.dot(hidden, out_w_ref[...], preferred_element_type=F32)
        more = row_ref[:, feat:].astype(F32)
        routes = pltpu.roll(more, LANES - TOP, 1)
        lane = lax.broadcasted_iota(jnp.int32, more.shape, 1)
        line = lax.broadcasted_iota(jnp.int32, more.shape, 0)
        target = jnp.where(line % (2 * each) < each, target_ref[0], target_ref[1]).astype(F32)
        chosen = (routes == target) & (lane < TOP)
        share = jnp.sum(jnp.where(chosen, more, 0.0), axis=1, keepdims=True)
        out_ref[...] = (result * share).astype(dtype)

    return pl.pallas_call(
        body,
        name="experts",
        out_shape=jax.ShapeDtypeStruct((count, feat), dtype),
        grid=(count // step,),
        in_specs=[
            pl.BlockSpec(memory_space=pltpu.SMEM),
            pl.BlockSpec((step, width), lambda i: (i, 0)),
            pl.BlockSpec(w_in.shape, lambda i: (0, 0)),
            pl.BlockSpec(w_out.shape, lambda i: (0, 0)),
        ],
        out_specs=pl.BlockSpec((step, feat), lambda i: (i, 0)),
        compiler_params=pltpu.CompilerParams(vmem_limit_bytes=48 * 1024 * 1024),
        cost_estimate=pl.CostEstimate(flops=0, bytes_accessed=0, transcendentals=0),
    )(targets, rows, w_in, w_out)


def a2a(x):
    return lax.all_to_all(x, "ep", split_axis=0, concat_axis=0, tiled=True)


def tiles(piece, pieces, unit, inner, columns):
    per_column = inner // unit
    for j in range(2 * inner // LANES):
        u = j * pieces + piece
        row = pl.multiple_of((u % per_column) * unit, unit)
        column = pl.multiple_of((u // per_column) * LANES, LANES)
        yield row, column, j * LANES


def pack(w_in, w_out, gi, part_rows, pieces):
    inner = w_out.shape[0]
    cut = part_rows // pieces
    unit = cut // 2
    step = 4

    def body(_, gate_ref, down_ref, out_ref):
        at = pl.program_id(0) * step
        for i in range(step):
            out_ref[i, :cut, :] = gate_ref[i * cut : (i + 1) * cut, :]
            for row, column, to in tiles(at + i, pieces, unit, inner, part_rows):
                out_ref[i, cut:, to : to + LANES] = down_ref[pl.ds(row, unit), pl.ds(column, LANES)]

    return pl.pallas_call(
        body,
        name="pack",
        out_shape=jax.ShapeDtypeStruct((pieces, cut + unit, 2 * inner), BF),
        grid_spec=pltpu.PrefetchScalarGridSpec(
            num_scalar_prefetch=1,
            grid=(pieces // step,),
            in_specs=[
                pl.BlockSpec((step * cut, 2 * inner), lambda p, g: (g[0] * (pieces // step) + p, 0)),
                pl.BlockSpec((inner, part_rows), lambda p, g: (0, g[0])),
            ],
            out_specs=pl.BlockSpec((step, cut + unit, 2 * inner), lambda p, g: (p, 0, 0)),
        ),
        compiler_params=pltpu.CompilerParams(vmem_limit_bytes=32 * 1024 * 1024),
        cost_estimate=pl.CostEstimate(
            flops=0, bytes_accessed=12 * part_rows * inner, transcendentals=0
        ),
    )(gi.reshape(1), w_in, w_out)


def unpack(packed, part_rows, inner):
    pieces = packed.shape[0]
    cut = part_rows // pieces
    unit = cut // 2
    step = 4

    def body(in_ref, gate_ref, down_ref):
        at = pl.program_id(0) * step
        for i in range(step):
            gate_ref[i * cut : (i + 1) * cut, :] = in_ref[i, :cut, :]
            for row, column, to in tiles(at + i, pieces, unit, inner, part_rows):
                down_ref[pl.ds(row, unit), pl.ds(column, LANES)] = in_ref[i, cut:, to : to + LANES]

    return pl.pallas_call(
        body,
        name="unpack",
        out_shape=[
            jax.ShapeDtypeStruct((part_rows, 2 * inner), BF),
            jax.ShapeDtypeStruct((inner, part_rows), BF),
        ],
        grid=(pieces // step,),
        in_specs=[pl.BlockSpec((step, cut + unit, 2 * inner), lambda p: (p, 0, 0))],
        out_specs=[
            pl.BlockSpec((step * cut, 2 * inner), lambda p: (p, 0)),
            pl.BlockSpec((inner, part_rows), lambda p: (0, 0)),
        ],
        compiler_params=pltpu.CompilerParams(vmem_limit_bytes=32 * 1024 * 1024),
        cost_estimate=pl.CostEstimate(
            flops=0, bytes_accessed=12 * part_rows * inner, transcendentals=0
        ),
    )(packed)


def local(
    tokens_one,
    routes_one,
    gates_one,
    tokens_two,
    routes_two,
    gates_two,
    old_table,
    new_table,
    gate_up,
    down_proj,
    norm_gain,
    kv_weight,
):
    w_in = gate_up[0]
    w_out = down_proj[0]
    ep = lax.axis_size("ep")
    grp = lax.axis_size("grp")
    me = lax.axis_index("ep")
    gi = lax.axis_index("grp")
    rows = tokens_one.shape[0]
    feat = w_in.shape[0]
    inner = w_out.shape[0]
    numbers = jnp.arange(ep, dtype=jnp.int32)
    sources_new = jnp.sum(
        (new_table[:, None] == old_table[None, :]).astype(jnp.int32) * numbers[None, :], axis=1
    )
    new_here = jnp.sum((sources_new == me).astype(jnp.int32) * numbers)

    mine = join(
        [(tokens_one, gates_one.T, routes_one.T), (tokens_two, gates_two.T, routes_two.T)]
    )
    far = [4 * i for i in range(1, ep // 4)]
    blocks = [mine] + [swap(mine, "ep", d) for d in far]

    part_rows = feat // grp
    cut = part_rows // ep
    packing = cut % 32 == 0 and inner % (cut // 2) == 0 and part_rows % LANES == 0 == inner % 64
    if packing:
        pieces = [pack(w_in, w_out, gi, part_rows, ep)]
    else:
        half_in = lax.dynamic_slice_in_dim(w_in, gi * part_rows, part_rows, 0)
        half_out = lax.dynamic_slice_in_dim(w_out, gi * part_rows, part_rows, 1)
        pieces = [half_in.reshape(ep, cut, 2 * inner), half_out.reshape(ep, inner // ep, part_rows)]
    near, pieces = lax.optimization_barrier((blocks[1], pieces))
    spread = [a2a(x) for x in pieces]
    line = jnp.concatenate([mine, near] + blocks[2:], axis=0)

    kv_blocks = [lax.optimization_barrier((kv_weight, line))[0]]
    for bit in range(grp.bit_length() - 1):
        kv_blocks = kv_blocks + [swap(x, "grp", 1 << bit) for x in kv_blocks]

    here = jnp.concatenate([line, swap(line, "ep", 2)], axis=0)
    there = swap(here, "ep", 1)
    targets = jnp.stack([me, new_here])
    kept = experts(here, rows, targets, w_in, w_out, F32)
    given = experts(there, rows, targets, w_in, w_out, BF)

    kept = kept + swap(given, "ep", 1).astype(F32)
    middle = kept.shape[0] // 2
    sent, wanted = lax.optimization_barrier((kept[middle:].astype(BF), sources_new))
    kept = kept[:middle] + swap(sent, "ep", 2).astype(F32)
    kept, wanted = lax.optimization_barrier((kept, wanted))
    block = 2 * rows
    sent = [kept[(i + 1) * block : (i + 2) * block].astype(BF) for i in range(len(far))]
    came = [swap(x, "ep", d) for x, d in zip(sent, far)]
    grouped = [x[wanted] for x in spread]
    came, grouped = lax.optimization_barrier((came, grouped))
    moved = [a2a(x) for x in grouped]
    mix = kept[:block] + sum(x.astype(F32) for x in came)
    own = jnp.concatenate([tokens_one, tokens_two], axis=0)
    hidden_all = (own.astype(F32) + mix).astype(BF)

    if packing:
        gate_up_new, down_proj_new = unpack(moved[0], part_rows, inner)
    else:
        gate_up_new = moved[0].reshape(part_rows, 2 * inner)
        down_proj_new = moved[1].reshape(inner, part_rows)

    normed = rms_norm(hidden_all, norm_gain)
    blocks = [jnp.dot(normed, w, preferred_element_type=F32).astype(BF) for w in kv_blocks]
    kv = jnp.take(jnp.stack(blocks), gi ^ jnp.arange(grp), axis=0)
    kv = kv.transpose(1, 0, 2).reshape(2 * rows, -1)
    return (
        hidden_all[:rows],
        kv[:rows],
        hidden_all[rows:],
        kv[rows:],
        gate_up_new[None],
        down_proj_new[None],
    )


def solution(mesh):
    tok = P(("grp", "ep"), None)
    return jax.shard_map(
        local,
        mesh=mesh,
        in_specs=(
            tok,
            tok,
            tok,
            tok,
            tok,
            tok,
            P(),
            P(),
            P("ep", None, None),
            P("ep", None, None),
            P(),
            P(None, "grp"),
        ),
        out_specs=(tok, tok, tok, tok, P("ep", "grp", None), P("ep", None, "grp")),
        check_vma=False,
    )
```

profile of v0, /device:TPU:13, one launch (start us, length us, event | category | flops | bytes accessed | tf_op | source)
XLA Modules:
  0.0 271.9 jit_solution(15477203960605052886)
XLA Ops:
  0.6 1.9 join.1
  2.7 2.3 collective-permute-start.1
  5.2 2.6 copy-done
  7.8 1.8 copy-done.1
  9.6 1.5 pack.1
  11.1 2.1 copy-done.3
  13.4 3.9 %collective-permute-done.1 = bf16[64,2176]{1,0:T(8,128)(2,1)S(1)} collective-permute-done((bf16[64,2176]{1,0:T(8,128)(2,1)}, bf16[64,2176]{1,0:T(8,128)(2,1)S(1)}, u32[]{:S(2)}, u32[]{:S(2)}) %collective-permute-start.1) | collective-permute-done | bytes 278560 | tf_op jit(solution)/shard_map/ppermute | solution.py:22
  17.3 11.9 %collective-permute-done.2 = bf16[64,2176]{1,0:T(8,128)(2,1)S(1)} collective-permute-done((bf16[64,2176]{1,0:T(8,128)(2,1)}, bf16[64,2176]{1,0:T(8,128)(2,1)S(1)}, u32[]{:S(2)}, u32[]{:S(2)}) %collective-permute-start.2) | collective-permute-done | bytes 278560 | tf_op jit(solution)/shard_map/ppermute | solution.py:22
  29.2 1.1 pad_maximum_fusion
  30.5 7.0 %all-to-all-start = ((bf16[16,96,1408]{2,1,0:T(8,128)(2,1)}), bf16[16,96,1408]{2,1,0:T(8,128)(2,1)}, u32[]{:S(2)}, u32[]{:S(2)}) async-start(bf16[16,96,1408]{2,1,0:T(8,128)(2,1)} %copy-done.3), calls=%async_computation | async-start | bytes 8650752 | tf_op jit(solution)/shard_map/all_to_all | solution.py:99
  37.6 28.8 %collective-permute-done.3 = bf16[256,2176]{1,0:T(8,128)(2,1)} collective-permute-done((bf16[256,2176]{1,0:T(8,128)(2,1)}, bf16[256,2176]{1,0:T(8,128)(2,1)}, u32[]{:S(2)}, u32[]{:S(2)}) %collective-permute-start.3) | collective-permute-done | bytes 1114144 | tf_op jit(solution)/shard_map/ppermute | solution.py:22
  66.4 1.4 constant_dynamic-update-slice_fusion.row_ref
  67.8 5.1 %collective-permute-start.4 = (bf16[512,2176]{1,0:T(8,128)(2,1)S(1)}, bf16[512,2176]{1,0:T(8,128)(2,1)}, u32[]{:S(2)}, u32[]{:S(2)}) collective-permute-start(bf16[512,2176]{1,0:T(8,128)(2,1)S(1)} %constant_dynamic-update-slice_fusion.row_ref), channel_id=1, source_target_pairs={{0,1},{1,0},{2,3},{3,2},{4,5},{5,4},{6,7},{7,6},{8,9},{9,8},{10,11... | collective-permute-start | bytes 6684680 | tf_op jit(solution)/shard_map/ppermute | solution.py:22
  73.1 0.6 fusion.7
  73.7 0.7 pad_add_fusion.target_ref
  74.4 2.6 collective-permute-done.4.row_ref
  77.0 9.3 %experts.3 = bf16[512,2048]{1,0:T(8,128)(2,1)S(1)} custom-call(s32[2]{0:T(128)S(1)} %pad_add_fusion.target_ref, bf16[512,2176]{1,0:T(8,128)(2,1)} %collective-permute-done.4.row_ref, bf16[2048,1408]{1,0:T(8,128)(2,1)} %bitcast.27, bf16[704,2048]{1,0:T(8,128)(2,1)} %bitcast.30), custom_call_target="tpu_custom_call" | custom-call | tf_op jit(solution)/shard_map/experts/pallas_call | solution.py:81
  86.7 9.5 %experts.2 = f32[512,2048]{1,0:T(8,128)} custom-call(s32[2]{0:T(128)S(1)} %pad_add_fusion.target_ref, bf16[512,2176]{1,0:T(8,128)(2,1)S(1)} %constant_dynamic-update-slice_fusion.row_ref, bf16[2048,1408]{1,0:T(8,128)(2,1)} %bitcast.28, bf16[704,2048]{1,0:T(8,128)(2,1)S(1)} %bitcast.32), custom_call_target="tpu_custom_call" | custom-call | tf_op jit(solution)/shard_map/experts/pallas_call | solution.py:81
  96.2 2.9 %convert_add_fusion = f32[512,2048]{1,0:T(8,128)S(1)} fusion(f32[512,2048]{1,0:T(8,128)} %experts.2, bf16[512,2048]{1,0:T(8,128)(2,1)S(1)} %collective-permute-done.5), kind=kLoop, calls=%fused_computation.2 | loop fusion | flops 2097152 | bytes 10485760 | tf_op jit(solution)/shard_map/add | solution.py:235
  99.3 36.2 %collective-permute-done.6 = bf16[256,2048]{1,0:T(8,128)(2,1)S(1)} collective-permute-done((bf16[256,2048]{1,0:T(8,128)(2,1)S(1)}, bf16[256,2048]{1,0:T(8,128)(2,1)S(1)}, u32[]{:S(2)}, u32[]{:S(2)}) %collective-permute-start.6) | collective-permute-done | bytes 1048608 | tf_op jit(solution)/shard_map/ppermute | solution.py:22
  135.9 0.9 fusion.9
  136.8 5.0 %collective-permute-start.8 = (bf16[64,2048]{1,0:T(8,128)(2,1)}, bf16[64,2048]{1,0:T(8,128)(2,1)S(1)}, u32[]{:S(2)}, u32[]{:S(2)}) collective-permute-start(bf16[64,2048]{1,0:T(8,128)(2,1)} %get-tuple-element.35), channel_id=1, source_target_pairs={{0,8},{1,9},{2,10},{3,11},{4,12},{5,13},{6,14},{7,15},{8,0},{9,1},... | collective-permute-start | bytes 786440 | tf_op jit(solution)/shard_map/ppermute | solution.py:22
  141.8 5.3 %gather_fusion = bf16[16,96,1408]{2,1,0:T(8,128)(2,1)} fusion(bf16[16,96,1408]{2,1,0:T(8,128)(2,1)} %all-to-all-done, s32[1024]{0:T(1024)S(1)} %pad_clamp_fusion.1), kind=kCustom, calls=%fused_computation | custom fusion | bytes 8650816 | tf_op jit(solution)/shard_map/gather | solution.py:243
  147.4 11.2 %collective-permute-done.8 = bf16[64,2048]{1,0:T(8,128)(2,1)S(1)} collective-permute-done((bf16[64,2048]{1,0:T(8,128)(2,1)}, bf16[64,2048]{1,0:T(8,128)(2,1)S(1)}, u32[]{:S(2)}, u32[]{:S(2)}) %collective-permute-start.8) | collective-permute-done | bytes 262176 | tf_op jit(solution)/shard_map/ppermute | solution.py:22
  158.6 5.5 %collective-permute-done.9 = bf16[64,2048]{1,0:T(8,128)(2,1)S(1)} collective-permute-done((bf16[64,2048]{1,0:T(8,128)(2,1)S(1)}, bf16[64,2048]{1,0:T(8,128)(2,1)S(1)}, u32[]{:S(2)}, u32[]{:S(2)}) %collective-permute-start.9) | collective-permute-done | bytes 262176 | tf_op jit(solution)/shard_map/ppermute | solution.py:22
  164.1 7.0 %all-to-all-start.1 = ((bf16[16,96,1408]{2,1,0:T(8,128)(2,1)}), bf16[16,96,1408]{2,1,0:T(8,128)(2,1)}, u32[]{:S(2)}, u32[]{:S(2)}) async-start(bf16[16,96,1408]{2,1,0:T(8,128)(2,1)} %gather_fusion), calls=%async_computation.1 | async-start | bytes 8650752 | tf_op jit(solution)/shard_map/all_to_all | solution.py:99
  171.1 1.2 collective-permute-start.10
  172.7 2.1 fusion
  174.8 43.5 %collective-permute-done.10 = bf16[2048,512]{1,0:T(8,128)(2,1)S(1)} collective-permute-done((bf16[2048,512]{1,0:T(8,128)(2,1)}, bf16[2048,512]{1,0:T(8,128)(2,1)S(1)}, u32[]{:S(2)}, u32[]{:S(2)}) %collective-permute-start.10) | collective-permute-done | bytes 2097184 | tf_op jit(solution)/shard_map/ppermute | solution.py:22
  220.8 0.7 fusion.10
  221.5 44.9 %all-to-all-done.1.in_ref = bf16[16,96,1408]{2,1,0:T(8,128)(2,1)} async-done(((bf16[16,96,1408]{2,1,0:T(8,128)(2,1)}), bf16[16,96,1408]{2,1,0:T(8,128)(2,1)}, u32[]{:S(2)}, u32[]{:S(2)}) %all-to-all-start.1) | async-done | bytes 4325408 | tf_op jit(solution)/shard_map/all_to_all | solution.py:99
  266.4 5.5 %unpack.1 = (bf16[1024,1408]{1,0:T(8,128)(2,1)}, bf16[704,1024]{1,0:T(8,128)(2,1)}) custom-call(bf16[16,96,1408]{2,1,0:T(8,128)(2,1)} %all-to-all-done.1.in_ref), custom_call_target="tpu_custom_call" | custom-call | bytes 8650752 | tf_op jit(solution)/shard_map/unpack/pallas_call | solution.py:157
  (51 shorter events, 5.3 us)
Async XLA Ops:
  2.5 10.9 %collective-permute-start = (bf16[64,2176]{1,0:T(8,128)(2,1)}, bf16[64,2176]{1,0:T(8,128)(2,1)S(1)}, u32[]{:S(2)}, u32[]{:S(2)}) collective-permute-start(bf16[64,2176]{1,0:T(8,128)(2,1)} %join.1), channel_id=1, source_target_pairs={{0,4},{1,5},{2,6},{3,7},{4,0},{5,1},{6,2},{7,3},{8,12},{9,13},{10,... | collective-permute-start | bytes 835592 | tf_op jit(solution)/shard_map/ppermute | solution.py:22
  2.7 14.6 %collective-permute-start.1 = (bf16[64,2176]{1,0:T(8,128)(2,1)}, bf16[64,2176]{1,0:T(8,128)(2,1)S(1)}, u32[]{:S(2)}, u32[]{:S(2)}) collective-permute-start(bf16[64,2176]{1,0:T(8,128)(2,1)} %join.1), channel_id=1, source_target_pairs={{0,8},{1,9},{2,10},{3,11},{4,12},{5,13},{6,14},{7,15},{8,0},{9,1},... | collective-permute-start | bytes 835592 | tf_op jit(solution)/shard_map/ppermute | solution.py:22
  5.0 24.2 %collective-permute-start.2 = (bf16[64,2176]{1,0:T(8,128)(2,1)}, bf16[64,2176]{1,0:T(8,128)(2,1)S(1)}, u32[]{:S(2)}, u32[]{:S(2)}) collective-permute-start(bf16[64,2176]{1,0:T(8,128)(2,1)} %join.1), channel_id=1, source_target_pairs={{0,12},{1,13},{2,14},{3,15},{4,8},{5,9},{6,10},{7,11},{8,4},{9,5},... | collective-permute-start | bytes 835592 | tf_op jit(solution)/shard_map/ppermute | solution.py:22
  5.2 2.6 copy-start
  7.8 1.8 copy-start.1
  9.6 19.5 %copy-start.4 = (bf16[64,2176]{1,0:T(8,128)(2,1)S(1)}, bf16[64,2176]{1,0:T(8,128)(2,1)}, u32[]{:S(2)}) copy-start(bf16[64,2176]{1,0:T(8,128)(2,1)} %join.1) | copy-start | bytes 835588
  11.1 2.1 copy-start.3
  30.2 36.2 %collective-permute-start.3 = (bf16[256,2176]{1,0:T(8,128)(2,1)}, bf16[256,2176]{1,0:T(8,128)(2,1)}, u32[]{:S(2)}, u32[]{:S(2)}) collective-permute-start(bf16[256,2176]{1,0:T(8,128)(2,1)} %pad_maximum_fusion), channel_id=1, source_target_pairs={{0,2},{1,3},{2,0},{3,1},{4,6},{5,7},{6,4},{7,5},{8,10},{9,11},{10,... | collective-permute-start | bytes 3342344 | tf_op jit(solution)/shard_map/ppermute | solution.py:22
  30.5 111.3 %all-to-all-start = ((bf16[16,96,1408]{2,1,0:T(8,128)(2,1)}), bf16[16,96,1408]{2,1,0:T(8,128)(2,1)}, u32[]{:S(2)}, u32[]{:S(2)}) async-start(bf16[16,96,1408]{2,1,0:T(8,128)(2,1)} %copy-done.3), calls=%async_computation | async-start | bytes 8650752 | tf_op jit(solution)/shard_map/all_to_all | solution.py:99
  37.5 35.4 %copy-start.8 = (s32[16]{0:T(128)S(1)}, s32[16]{0:T(128)}, u32[]{:S(2)}) copy-start(s32[16]{0:T(128)} %param.18) | copy-start | bytes 196
  37.5 35.4 %copy-start.9 = (s32[16]{0:T(128)S(1)}, s32[16]{0:T(128)}, u32[]{:S(2)}) copy-start(s32[16]{0:T(128)} %param.19) | copy-start | bytes 196
  67.8 9.2 %collective-permute-start.4 = (bf16[512,2176]{1,0:T(8,128)(2,1)S(1)}, bf16[512,2176]{1,0:T(8,128)(2,1)}, u32[]{:S(2)}, u32[]{:S(2)}) collective-permute-start(bf16[512,2176]{1,0:T(8,128)(2,1)S(1)} %constant_dynamic-update-slice_fusion.row_ref), channel_id=1, source_target_pairs={{0,1},{1,0},{2,3},{3,2},{4,5},{5,4},{6,7},{7,6},{8,9},{9,8},{10,11... | collective-permute-start | bytes 6684680 | tf_op jit(solution)/shard_map/ppermute | solution.py:22
  74.4 12.3 %copy-start.2 = (bf16[1,704,2048]{2,1,0:T(8,128)(2,1)S(1)}, bf16[1,704,2048]{2,1,0:T(8,128)(2,1)}, u32[]{:S(2)}) copy-start(bf16[1,704,2048]{2,1,0:T(8,128)(2,1)} %param.21) | copy-start | bytes 8650756
  86.3 9.9 %collective-permute-start.5 = (bf16[512,2048]{1,0:T(8,128)(2,1)S(1)}, bf16[512,2048]{1,0:T(8,128)(2,1)S(1)}, u32[]{:S(2)}, u32[]{:S(2)}) collective-permute-start(bf16[512,2048]{1,0:T(8,128)(2,1)S(1)} %experts.3), channel_id=1, source_target_pairs={{0,1},{1,0},{2,3},{3,2},{4,5},{5,4},{6,7},{7,6},{8,9},{9,8},{10,11... | collective-permute-start | bytes 6291464 | tf_op jit(solution)/shard_map/ppermute | solution.py:22
  99.2 36.3 %collective-permute-start.6 = (bf16[256,2048]{1,0:T(8,128)(2,1)S(1)}, bf16[256,2048]{1,0:T(8,128)(2,1)S(1)}, u32[]{:S(2)}, u32[]{:S(2)}) collective-permute-start(bf16[256,2048]{1,0:T(8,128)(2,1)S(1)} %slice.70), channel_id=1, source_target_pairs={{0,2},{1,3},{2,0},{3,1},{4,6},{5,7},{6,4},{7,5},{8,10},{9,11},{10,... | collective-permute-start | bytes 3145736 | tf_op jit(solution)/shard_map/ppermute | solution.py:22
  136.8 10.6 %collective-permute-start.7 = (bf16[64,2048]{1,0:T(8,128)(2,1)}, bf16[64,2048]{1,0:T(8,128)(2,1)S(1)}, u32[]{:S(2)}, u32[]{:S(2)}) collective-permute-start(bf16[64,2048]{1,0:T(8,128)(2,1)} %get-tuple-element.36), channel_id=1, source_target_pairs={{0,4},{1,5},{2,6},{3,7},{4,0},{5,1},{6,2},{7,3},{8,12},{9,13},{10,... | collective-permute-start | bytes 786440 | tf_op jit(solution)/shard_map/ppermute | solution.py:22
  136.8 21.8 %collective-permute-start.8 = (bf16[64,2048]{1,0:T(8,128)(2,1)}, bf16[64,2048]{1,0:T(8,128)(2,1)S(1)}, u32[]{:S(2)}, u32[]{:S(2)}) collective-permute-start(bf16[64,2048]{1,0:T(8,128)(2,1)} %get-tuple-element.35), channel_id=1, source_target_pairs={{0,8},{1,9},{2,10},{3,11},{4,12},{5,13},{6,14},{7,15},{8,0},{9,1},... | collective-permute-start | bytes 786440 | tf_op jit(solution)/shard_map/ppermute | solution.py:22
  141.8 22.4 %collective-permute-start.9 = (bf16[64,2048]{1,0:T(8,128)(2,1)S(1)}, bf16[64,2048]{1,0:T(8,128)(2,1)S(1)}, u32[]{:S(2)}, u32[]{:S(2)}) collective-permute-start(bf16[64,2048]{1,0:T(8,128)(2,1)S(1)} %get-tuple-element.34), channel_id=1, source_target_pairs={{0,12},{1,13},{2,14},{3,15},{4,8},{5,9},{6,10},{7,11},{8,4},{9,5},... | collective-permute-start | bytes 786440 | tf_op jit(solution)/shard_map/ppermute | solution.py:22
  147.1 25.2 %copy-start.7 = (bf16[2048]{0:T(1024)(128)(2,1)S(1)}, bf16[2048]{0:T(1024)(128)(2,1)}, u32[]{:S(2)}) copy-start(bf16[2048]{0:T(1024)(128)(2,1)} %param.22) | copy-start | bytes 12292
  147.1 25.3 %copy-start.5 = (bf16[32,2048]{1,0:T(8,128)(2,1)S(1)}, bf16[32,2048]{1,0:T(8,128)(2,1)}, u32[]{:S(2)}) copy-start(bf16[32,2048]{1,0:T(8,128)(2,1)} %refs_0_.1) | copy-start | bytes 393220
  147.1 25.3 %copy-start.6 = (bf16[32,2048]{1,0:T(8,128)(2,1)S(1)}, bf16[32,2048]{1,0:T(8,128)(2,1)}, u32[]{:S(2)}) copy-start(bf16[32,2048]{1,0:T(8,128)(2,1)} %refs_3_.1) | copy-start | bytes 393220
  164.1 102.2 %all-to-all-start.1 = ((bf16[16,96,1408]{2,1,0:T(8,128)(2,1)}), bf16[16,96,1408]{2,1,0:T(8,128)(2,1)}, u32[]{:S(2)}, u32[]{:S(2)}) async-start(bf16[16,96,1408]{2,1,0:T(8,128)(2,1)} %gather_fusion), calls=%async_computation.1 | async-start | bytes 8650752 | tf_op jit(solution)/shard_map/all_to_all | solution.py:99
  171.1 47.2 %collective-permute-start.10 = (bf16[2048,512]{1,0:T(8,128)(2,1)}, bf16[2048,512]{1,0:T(8,128)(2,1)S(1)}, u32[]{:S(2)}, u32[]{:S(2)}) collective-permute-start(bf16[2048,512]{1,0:T(8,128)(2,1)} %param.23), channel_id=1, source_target_pairs={{0,16},{16,0},{1,17},{17,1},{2,18},{18,2},{3,19},{19,3},{4,20},{20... | collective-permute-start | bytes 6291464 | tf_op jit(solution)/shard_map/ppermute | solution.py:22
where the time goes:
time: 273 us; the launch traced here: 272 us
  waiting for transfers between devices  189 us (69%)
  starting transfers between devices  28.7 us (11%)
  Pallas kernels  27.7 us (10%)
  local copies, waits for them, and re-layouts  16.9 us (6%)
  other arithmetic  6.31 us (2%)
    ppermute x11, waiting for transfers between devices, swap(): return lax.ppermute(x, axis, [(i, i ^ distance) for i in range(size)])  144 us
    all_to_all x2, waiting for transfers between devices, a2a(): return lax.all_to_all(x, 'ep', split_axis=0, concat_axis=0, tiled=True)  44.9 us
    pallas_call x2, Pallas kernels, experts(): pl.pallas_call(body, name='experts', out_shape=jax.ShapeDtypeStruct((coun...  18.8 us
    ppermute x11, starting transfers between devices, swap(): return lax.ppermute(x, axis, [(i, i ^ distance) for i in range(size)])  14.7 us
    all_to_all x2, starting transfers between devices, a2a(): return lax.all_to_all(x, 'ep', split_axis=0, concat_axis=0, tiled=True)  14 us
    unnamed x25, local copies, waits for them, and re-layouts  6.65 us
    pallas_call x1, Pallas kernels, unpack(): pl.pallas_call(body, name='unpack', out_shape=[jax.ShapeDtypeStruct((part...  5.54 us
  transfers between devices with their start and end apart: 13, of which 11 were waited for; matrix products, arithmetic and copies ran while one was open for 7% of the time, Pallas kernels for 7%

commit v1 on v0

--- a/solution.py
+++ b/solution.py
@@ -57,42 +57,48 @@
     )(*[x for part in parts for x in part])
 
 
-def experts(rows, each, targets, w_in, w_out, dtype):
+def experts(here, there, half, each, targets, w_in, w_out):
     inner, feat = w_out.shape
-    count = rows.shape[0]
-    width = rows.shape[1]
+    count = here.shape[0] // 2
+    width = here.shape[1]
     step = min(256, count)
 
-    def body(target_ref, row_ref, in_ref, out_w_ref, out_ref):
-        joined = jnp.dot(row_ref[:, :feat], in_ref[...], preferred_element_type=F32)
-        upward = pltpu.roll(joined, inner, 1)
-        hidden = joined / (1.0 + jnp.exp(-joined)) * upward
-        hidden = hidden[:, :inner].astype(BF)
-        result = jnp.dot(hidden, out_w_ref[...], preferred_element_type=F32)
-        more = row_ref[:, feat:].astype(F32)
-        routes = pltpu.roll(more, LANES - TOP, 1)
-        lane = lax.broadcasted_iota(jnp.int32, more.shape, 1)
-        line = lax.broadcasted_iota(jnp.int32, more.shape, 0)
-        target = jnp.where(line % (2 * each) < each, target_ref[0], target_ref[1]).astype(F32)
-        chosen = (routes == target) & (lane < TOP)
-        share = jnp.sum(jnp.where(chosen, more, 0.0), axis=1, keepdims=True)
-        out_ref[...] = (result * share).astype(dtype)
-
+    def body(target_ref, here_ref, there_ref, in_ref, out_w_ref, kept_ref, given_ref):
+        for row_ref, out_ref in ((there_ref, given_ref), (here_ref, kept_ref)):
+            joined = jnp.dot(row_ref[:, :feat], in_ref[...], preferred_element_type=F32)
+            upward = pltpu.roll(joined, inner, 1)
+            hidden = joined / (1.0 + jnp.exp(-joined)) * upward
+            hidden = hidden[:, :inner].astype(BF)
+            result = jnp.dot(hidden, out_w_ref[...], preferred_element_type=F32)
+            more = row_ref[:, feat:].astype(F32)
+            routes = pltpu.roll(more, LANES - TOP, 1)
+            lane = lax.broadcasted_iota(jnp.int32, more.shape, 1)
+            line = lax.broadcasted_iota(jnp.int32, more.shape, 0)
+            target = jnp.where(line % (2 * each) < each, target_ref[0], target_ref[1])
+            chosen = (routes == target.astype(F32)) & (lane < TOP)
+            share = jnp.sum(jnp.where(chosen, more, 0.0), axis=1, keepdims=True)
+            out_ref[...] = (result * share).astype(out_ref.dtype)
+
+    first = half * (count // step)
     return pl.pallas_call(
         body,
         name="experts",
-        out_shape=jax.ShapeDtypeStruct((count, feat), dtype),
+        out_shape=[
+            jax.ShapeDtypeStruct((count, feat), F32),
+            jax.ShapeDtypeStruct((count, feat), BF),
+        ],
         grid=(count // step,),
         in_specs=[
             pl.BlockSpec(memory_space=pltpu.SMEM),
-            pl.BlockSpec((step, width), lambda i: (i, 0)),
+            pl.BlockSpec((step, width), lambda i: (first + i, 0)),
+            pl.BlockSpec((step, width), lambda i: (first + i, 0)),
             pl.BlockSpec(w_in.shape, lambda i: (0, 0)),
             pl.BlockSpec(w_out.shape, lambda i: (0, 0)),
         ],
-        out_specs=pl.BlockSpec((step, feat), lambda i: (i, 0)),
+        out_specs=[pl.BlockSpec((step, feat), lambda i: (i, 0))] * 2,
         compiler_params=pltpu.CompilerParams(vmem_limit_bytes=48 * 1024 * 1024),
         cost_estimate=pl.CostEstimate(flops=0, bytes_accessed=0, transcendentals=0),
-    )(targets, rows, w_in, w_out)
+    )(targets, here, there, w_in, w_out)
 
 
 def a2a(x):
@@ -229,13 +235,13 @@
     here = jnp.concatenate([line, swap(line, "ep", 2)], axis=0)
     there = swap(here, "ep", 1)
     targets = jnp.stack([me, new_here])
-    kept = experts(here, rows, targets, w_in, w_out, F32)
-    given = experts(there, rows, targets, w_in, w_out, BF)
-
-    kept = kept + swap(given, "ep", 1).astype(F32)
-    middle = kept.shape[0] // 2
-    sent, wanted = lax.optimization_barrier((kept[middle:].astype(BF), sources_new))
-    kept = kept[:middle] + swap(sent, "ep", 2).astype(F32)
+
+    kept, given = experts(here, there, 1, rows, targets, w_in, w_out)
+    sent = (kept + swap(given, "ep", 1).astype(F32)).astype(BF)
+    sent, here, wanted = lax.optimization_barrier((sent, here, sources_new))
+    came = swap(sent, "ep", 2)
+    kept, given = experts(here, there, 0, rows, targets, w_in, w_out)
+    kept = kept + swap(given, "ep", 1).astype(F32) + came.astype(F32)
     kept, wanted = lax.optimization_barrier((kept, wanted))
     block = 2 * rows
     sent = [kept[(i + 1) * block : (i + 2) * block].astype(BF) for i in range(len(far))]

time: 273 us -> 279 us (1.022)
  waiting for transfers between devices: 189 us -> 199 us
  other arithmetic: 6.31 us -> 2.91 us
    ppermute x11 -> x12, waiting for transfers between devices: 144 us -> 154 us  [swap(): return lax.ppermute(x, axis, [(i, i ^ distance) for i in range(size)])]
    ppermute x11 -> x12, starting transfers between devices: 14.7 us -> 16.5 us  [swap(): return lax.ppermute(x, axis, [(i, i ^ distance) for i in range(size)])]
    unnamed x25 -> x23, local copies, waits for them, and re-layouts: 6.65 us -> 6.66 us
  transfers between devices with their start and end apart: 13 -> 14, of which waited for: 11 -> 11; matrix products, arithmetic and copies ran while one was open for 7% -> 5% of each run, Pallas kernels for 7% -> 7%
where the time goes in v1:
time: 279 us
  waiting for transfers between devices  199 us (71%)
  starting transfers between devices  30.8 us (11%)
  Pallas kernels  27.2 us (10%)
  local copies, waits for them, and re-layouts  15.5 us (6%)
  other arithmetic  2.91 us (1%)
    ppermute x12, waiting for transfers between devices, swap(): return lax.ppermute(x, axis, [(i, i ^ distance) for i in range(size)])  154 us
    all_to_all x2, waiting for transfers between devices, a2a(): return lax.all_to_all(x, 'ep', split_axis=0, concat_axis=0, tiled=True)  45.3 us
    pallas_call x2, Pallas kernels, experts(): pl.pallas_call(body, name='experts', out_shape=[jax.ShapeDtypeStruct((cou...  18.3 us
    ppermute x12, starting transfers between devices, swap(): return lax.ppermute(x, axis, [(i, i ^ distance) for i in range(size)])  16.5 us
    all_to_all x2, starting transfers between devices, a2a(): return lax.all_to_all(x, 'ep', split_axis=0, concat_axis=0, tiled=True)  14.3 us
    unnamed x23, local copies, waits for them, and re-layouts  6.66 us
  transfers between devices with their start and end apart: 14, of which 11 were waited for; matrix products, arithmetic and copies ran while one was open for 5% of the time, Pallas kernels for 7%

profile of v1, /device:TPU:13, one launch (start us, length us, event | category | flops | bytes accessed | tf_op | source)
XLA Modules:
  0.0 278.8 jit_solution(11377630907532232782)
XLA Ops:
  0.6 1.9 join.1
  2.7 2.3 collective-permute-start.1
  5.2 2.6 copy-done
  7.8 1.8 copy-done.1
  9.6 1.5 pack.1
  11.1 2.1 copy-done.2
  13.4 8.9 %all-to-all-start = ((bf16[16,96,1408]{2,1,0:T(8,128)(2,1)}), bf16[16,96,1408]{2,1,0:T(8,128)(2,1)}, u32[]{:S(2)}, u32[]{:S(2)}) async-start(bf16[16,96,1408]{2,1,0:T(8,128)(2,1)} %copy-done.2), calls=%async_computation | async-start | bytes 8650752 | tf_op jit(solution)/shard_map/all_to_all | solution.py:105
  22.3 24.3 %collective-permute-done.2 = bf16[64,2176]{1,0:T(8,128)(2,1)S(1)} collective-permute-done((bf16[64,2176]{1,0:T(8,128)(2,1)}, bf16[64,2176]{1,0:T(8,128)(2,1)S(1)}, u32[]{:S(2)}, u32[]{:S(2)}) %collective-permute-start.2) | collective-permute-done | bytes 278560 | tf_op jit(solution)/shard_map/ppermute | solution.py:22
  46.7 6.0 %collective-permute-start.3 = (bf16[256,2176]{1,0:T(8,128)(2,1)S(1)}, bf16[256,2176]{1,0:T(8,128)(2,1)S(1)}, u32[]{:S(2)}, u32[]{:S(2)}) collective-permute-start(bf16[256,2176]{1,0:T(8,128)(2,1)S(1)} %pad_maximum_fusion), channel_id=1, source_target_pairs={{0,2},{1,3},{2,0},{3,1},{4,6},{5,7},{6,4},{7,5},{8,10},{9,11},{10,... | collective-permute-start | bytes 3342344 | tf_op jit(solution)/shard_map/ppermute | solution.py:22
  52.8 46.2 %collective-permute-done.3 = bf16[256,2176]{1,0:T(8,128)(2,1)S(1)} collective-permute-done((bf16[256,2176]{1,0:T(8,128)(2,1)S(1)}, bf16[256,2176]{1,0:T(8,128)(2,1)S(1)}, u32[]{:S(2)}, u32[]{:S(2)}) %collective-permute-start.3) | collective-permute-done | bytes 1114144 | tf_op jit(solution)/shard_map/ppermute | solution.py:22
  99.9 0.6 fusion.7
  100.6 0.7 pad_add_fusion.target_ref
  101.3 2.6 collective-permute-done.4.there_ref
  103.9 9.2 %experts.2 = (f32[256,2048]{1,0:T(8,128)S(1)}, bf16[256,2048]{1,0:T(8,128)(2,1)S(1)}) custom-call(s32[2]{0:T(128)S(1)} %pad_add_fusion.target_ref, bf16[512,2176]{1,0:T(8,128)(2,1)S(1)} %constant_dynamic-update-slice_fusion.here_ref, bf16[512,2176]{1,0:T(8,128)(2,1)} %collective-permute-done.4.there_ref, bf16[2048,1408]{1,0:T(8,128)(2,1)} %bitcast.27, ...), custom_call_target="tpu_custom_call" | custom-call | tf_op jit(solution)/shard_map/experts/pallas_call | solution.py:83
  113.5 2.3 collective-permute-done.5
  116.0 2.3 collective-permute-start.7
  118.3 9.2 %experts.3 = (f32[256,2048]{1,0:T(8,128)S(1)}, bf16[256,2048]{1,0:T(8,128)(2,1)S(1)}) custom-call(s32[2]{0:T(128)S(1)} %pad_add_fusion.target_ref, bf16[512,2176]{1,0:T(8,128)(2,1)S(1)} %constant_dynamic-update-slice_fusion.here_ref, bf16[512,2176]{1,0:T(8,128)(2,1)} %collective-permute-done.4.there_ref, bf16[2048,1408]{1,0:T(8,128)(2,1)} %bitcast.28, ...), custom_call_target="tpu_custom_call" | custom-call | tf_op jit(solution)/shard_map/experts/pallas_call | solution.py:83
  127.5 0.7 collective-permute-start.6
  128.2 17.5 %collective-permute-done.7 = bf16[256,2048]{1,0:T(8,128)(2,1)S(1)} collective-permute-done((bf16[256,2048]{1,0:T(8,128)(2,1)S(1)}, bf16[256,2048]{1,0:T(8,128)(2,1)S(1)}, u32[]{:S(2)}, u32[]{:S(2)}) %collective-permute-start.7) | collective-permute-done | bytes 1048608 | tf_op jit(solution)/shard_map/ppermute | solution.py:22
  146.3 0.9 fusion.9
  147.6 2.2 collective-permute-start.10
  149.8 5.3 %gather_fusion = bf16[16,96,1408]{2,1,0:T(8,128)(2,1)} fusion(bf16[16,96,1408]{2,1,0:T(8,128)(2,1)} %all-to-all-done, s32[1024]{0:T(1024)S(1)} %pad_clamp_fusion.1), kind=kCustom, calls=%fused_computation | custom fusion | bytes 8650816 | tf_op jit(solution)/shard_map/gather | solution.py:249
  155.1 1.3 collective-permute-done.8
  156.5 2.7 collective-permute-done.9
  159.2 13.5 %collective-permute-done.10 = bf16[64,2048]{1,0:T(8,128)(2,1)S(1)} collective-permute-done((bf16[64,2048]{1,0:T(8,128)(2,1)S(1)}, bf16[64,2048]{1,0:T(8,128)(2,1)S(1)}, u32[]{:S(2)}, u32[]{:S(2)}) %collective-permute-start.10) | collective-permute-done | bytes 262176 | tf_op jit(solution)/shard_map/ppermute | solution.py:22
  172.6 5.4 %all-to-all-start.1 = ((bf16[16,96,1408]{2,1,0:T(8,128)(2,1)}), bf16[16,96,1408]{2,1,0:T(8,128)(2,1)}, u32[]{:S(2)}, u32[]{:S(2)}) async-start(bf16[16,96,1408]{2,1,0:T(8,128)(2,1)} %gather_fusion), calls=%async_computation.1 | async-start | bytes 8650752 | tf_op jit(solution)/shard_map/all_to_all | solution.py:105
  178.0 1.2 collective-permute-start.11
  179.6 2.1 fusion
  181.7 43.1 %collective-permute-done.11 = bf16[2048,512]{1,0:T(8,128)(2,1)S(1)} collective-permute-done((bf16[2048,512]{1,0:T(8,128)(2,1)}, bf16[2048,512]{1,0:T(8,128)(2,1)S(1)}, u32[]{:S(2)}, u32[]{:S(2)}) %collective-permute-start.11) | collective-permute-done | bytes 2097184 | tf_op jit(solution)/shard_map/ppermute | solution.py:22
  227.3 0.7 fusion.10
  228.0 45.3 %all-to-all-done.1.in_ref = bf16[16,96,1408]{2,1,0:T(8,128)(2,1)} async-done(((bf16[16,96,1408]{2,1,0:T(8,128)(2,1)}), bf16[16,96,1408]{2,1,0:T(8,128)(2,1)}, u32[]{:S(2)}, u32[]{:S(2)}) %all-to-all-start.1) | async-done | bytes 4325408 | tf_op jit(solution)/shard_map/all_to_all | solution.py:105
  273.3 5.5 %unpack.1 = (bf16[1024,1408]{1,0:T(8,128)(2,1)}, bf16[704,1024]{1,0:T(8,128)(2,1)}) custom-call(bf16[16,96,1408]{2,1,0:T(8,128)(2,1)} %all-to-all-done.1.in_ref), custom_call_target="tpu_custom_call" | custom-call | bytes 8650752 | tf_op jit(solution)/shard_map/unpack/pallas_call | solution.py:163
  (50 shorter events, 6.1 us)
Async XLA Ops:
  2.5 10.9 %collective-permute-start = (bf16[64,2176]{1,0:T(8,128)(2,1)}, bf16[64,2176]{1,0:T(8,128)(2,1)S(1)}, u32[]{:S(2)}, u32[]{:S(2)}) collective-permute-start(bf16[64,2176]{1,0:T(8,128)(2,1)} %join.1), channel_id=1, source_target_pairs={{0,4},{1,5},{2,6},{3,7},{4,0},{5,1},{6,2},{7,3},{8,12},{9,13},{10,... | collective-permute-start | bytes 835592 | tf_op jit(solution)/shard_map/ppermute | solution.py:22
  2.7 19.6 %collective-permute-start.1 = (bf16[64,2176]{1,0:T(8,128)(2,1)}, bf16[64,2176]{1,0:T(8,128)(2,1)S(1)}, u32[]{:S(2)}, u32[]{:S(2)}) collective-permute-start(bf16[64,2176]{1,0:T(8,128)(2,1)} %join.1), channel_id=1, source_target_pairs={{0,8},{1,9},{2,10},{3,11},{4,12},{5,13},{6,14},{7,15},{8,0},{9,1},... | collective-permute-start | bytes 835592 | tf_op jit(solution)/shard_map/ppermute | solution.py:22
  5.0 41.6 %collective-permute-start.2 = (bf16[64,2176]{1,0:T(8,128)(2,1)}, bf16[64,2176]{1,0:T(8,128)(2,1)S(1)}, u32[]{:S(2)}, u32[]{:S(2)}) collective-permute-start(bf16[64,2176]{1,0:T(8,128)(2,1)} %join.1), channel_id=1, source_target_pairs={{0,12},{1,13},{2,14},{3,15},{4,8},{5,9},{6,10},{7,11},{8,4},{9,5},... | collective-permute-start | bytes 835592 | tf_op jit(solution)/shard_map/ppermute | solution.py:22
  5.2 2.6 copy-start
  7.8 1.8 copy-start.1
  11.1 2.1 copy-start.2
  13.2 33.4 %copy-start.3 = (bf16[64,2176]{1,0:T(8,128)(2,1)S(1)}, bf16[64,2176]{1,0:T(8,128)(2,1)}, u32[]{:S(2)}) copy-start(bf16[64,2176]{1,0:T(8,128)(2,1)} %join.1) | copy-start | bytes 835588
  13.4 136.4 %all-to-all-start = ((bf16[16,96,1408]{2,1,0:T(8,128)(2,1)}), bf16[16,96,1408]{2,1,0:T(8,128)(2,1)}, u32[]{:S(2)}, u32[]{:S(2)}) async-start(bf16[16,96,1408]{2,1,0:T(8,128)(2,1)} %copy-done.2), calls=%async_computation | async-start | bytes 8650752 | tf_op jit(solution)/shard_map/all_to_all | solution.py:105
  46.7 53.0 %copy-start.7 = (s32[16]{0:T(128)S(1)}, s32[16]{0:T(128)}, u32[]{:S(2)}) copy-start(s32[16]{0:T(128)} %param.18) | copy-start | bytes 196
  46.7 53.0 %copy-start.8 = (s32[16]{0:T(128)S(1)}, s32[16]{0:T(128)}, u32[]{:S(2)}) copy-start(s32[16]{0:T(128)} %param.19) | copy-start | bytes 196
  46.7 52.3 %collective-permute-start.3 = (bf16[256,2176]{1,0:T(8,128)(2,1)S(1)}, bf16[256,2176]{1,0:T(8,128)(2,1)S(1)}, u32[]{:S(2)}, u32[]{:S(2)}) collective-permute-start(bf16[256,2176]{1,0:T(8,128)(2,1)S(1)} %pad_maximum_fusion), channel_id=1, source_target_pairs={{0,2},{1,3},{2,0},{3,1},{4,6},{5,7},{6,4},{7,5},{8,10},{9,11},{10,... | collective-permute-start | bytes 3342344 | tf_op jit(solution)/shard_map/ppermute | solution.py:22
  99.2 4.7 %collective-permute-start.4 = (bf16[512,2176]{1,0:T(8,128)(2,1)S(1)}, bf16[512,2176]{1,0:T(8,128)(2,1)}, u32[]{:S(2)}, u32[]{:S(2)}) collective-permute-start(bf16[512,2176]{1,0:T(8,128)(2,1)S(1)} %constant_dynamic-update-slice_fusion.here_ref), channel_id=1, source_target_pairs={{0,1},{1,0},{2,3},{3,2},{4,5},{5,4},{6,7},{7,6},{8,9},{9,8},{10,11... | collective-permute-start | bytes 6684680 | tf_op jit(solution)/shard_map/ppermute | solution.py:22
  113.0 2.7 collective-permute-start.5
  116.0 29.7 %collective-permute-start.7 = (bf16[256,2048]{1,0:T(8,128)(2,1)S(1)}, bf16[256,2048]{1,0:T(8,128)(2,1)S(1)}, u32[]{:S(2)}, u32[]{:S(2)}) collective-permute-start(bf16[256,2048]{1,0:T(8,128)(2,1)S(1)} %add_convert_fusion), channel_id=1, source_target_pairs={{0,2},{1,3},{2,0},{3,1},{4,6},{5,7},{6,4},{7,5},{8,10},{9,11},{10,... | collective-permute-start | bytes 3145736 | tf_op jit(solution)/shard_map/ppermute | solution.py:22
  127.5 18.2 %collective-permute-start.6 = (bf16[256,2048]{1,0:T(8,128)(2,1)S(1)}, bf16[256,2048]{1,0:T(8,128)(2,1)S(1)}, u32[]{:S(2)}, u32[]{:S(2)}) collective-permute-start(bf16[256,2048]{1,0:T(8,128)(2,1)S(1)} %get-tuple-element.29), channel_id=1, source_target_pairs={{0,1},{1,0},{2,3},{3,2},{4,5},{5,4},{6,7},{7,6},{8,9},{9,8},{10,11... | collective-permute-start | bytes 3145736 | tf_op jit(solution)/shard_map/ppermute | solution.py:22
  147.2 9.3 %collective-permute-start.8 = (bf16[64,2048]{1,0:T(8,128)(2,1)}, bf16[64,2048]{1,0:T(8,128)(2,1)S(1)}, u32[]{:S(2)}, u32[]{:S(2)}) collective-permute-start(bf16[64,2048]{1,0:T(8,128)(2,1)} %get-tuple-element.46), channel_id=1, source_target_pairs={{0,4},{1,5},{2,6},{3,7},{4,0},{5,1},{6,2},{7,3},{8,12},{9,13},{10,... | collective-permute-start | bytes 786440 | tf_op jit(solution)/shard_map/ppermute | solution.py:22
  147.2 12.0 %collective-permute-start.9 = (bf16[64,2048]{1,0:T(8,128)(2,1)}, bf16[64,2048]{1,0:T(8,128)(2,1)S(1)}, u32[]{:S(2)}, u32[]{:S(2)}) collective-permute-start(bf16[64,2048]{1,0:T(8,128)(2,1)} %get-tuple-element.45), channel_id=1, source_target_pairs={{0,8},{1,9},{2,10},{3,11},{4,12},{5,13},{6,14},{7,15},{8,0},{9,1},... | collective-permute-start | bytes 786440 | tf_op jit(solution)/shard_map/ppermute | solution.py:22
  147.6 25.0 %collective-permute-start.10 = (bf16[64,2048]{1,0:T(8,128)(2,1)S(1)}, bf16[64,2048]{1,0:T(8,128)(2,1)S(1)}, u32[]{:S(2)}, u32[]{:S(2)}) collective-permute-start(bf16[64,2048]{1,0:T(8,128)(2,1)S(1)} %get-tuple-element.44), channel_id=1, source_target_pairs={{0,12},{1,13},{2,14},{3,15},{4,8},{5,9},{6,10},{7,11},{8,4},{9,5},... | collective-permute-start | bytes 786440 | tf_op jit(solution)/shard_map/ppermute | solution.py:22
  155.1 24.1 %copy-start.6 = (bf16[2048]{0:T(1024)(128)(2,1)S(1)}, bf16[2048]{0:T(1024)(128)(2,1)}, u32[]{:S(2)}) copy-start(bf16[2048]{0:T(1024)(128)(2,1)} %param.22) | copy-start | bytes 12292
  155.1 24.1 %copy-start.4 = (bf16[32,2048]{1,0:T(8,128)(2,1)S(1)}, bf16[32,2048]{1,0:T(8,128)(2,1)}, u32[]{:S(2)}) copy-start(bf16[32,2048]{1,0:T(8,128)(2,1)} %refs_0_.1) | copy-start | bytes 393220
  155.1 24.1 %copy-start.5 = (bf16[32,2048]{1,0:T(8,128)(2,1)S(1)}, bf16[32,2048]{1,0:T(8,128)(2,1)}, u32[]{:S(2)}) copy-start(bf16[32,2048]{1,0:T(8,128)(2,1)} %refs_3_.1) | copy-start | bytes 393220
  172.6 100.7 %all-to-all-start.1 = ((bf16[16,96,1408]{2,1,0:T(8,128)(2,1)}), bf16[16,96,1408]{2,1,0:T(8,128)(2,1)}, u32[]{:S(2)}, u32[]{:S(2)}) async-start(bf16[16,96,1408]{2,1,0:T(8,128)(2,1)} %gather_fusion), calls=%async_computation.1 | async-start | bytes 8650752 | tf_op jit(solution)/shard_map/all_to_all | solution.py:105
  178.0 46.8 %collective-permute-start.11 = (bf16[2048,512]{1,0:T(8,128)(2,1)}, bf16[2048,512]{1,0:T(8,128)(2,1)S(1)}, u32[]{:S(2)}, u32[]{:S(2)}) collective-permute-start(bf16[2048,512]{1,0:T(8,128)(2,1)} %param.23), channel_id=1, source_target_pairs={{0,16},{16,0},{1,17},{17,1},{2,18},{18,2},{3,19},{19,3},{4,20},{20... | collective-permute-start | bytes 6291464 | tf_op jit(solution)/shard_map/ppermute | solution.py:22
